TPU v7x, 32 devices: a whole 2x2x4 slice. The times are simulated.
32 devices in a mesh: groups: 2 (over x), dp: 8 (over z, core), tensor: 2 (over y).
Axes of the slice: x: 2, y: 2, z: 4, core: 2. Of those that a mesh axis runs over, the one named last changes fastest.
Arguments:
- tokens: bfloat16 [4096, 8192], P(('groups', 'dp'), 'tensor'), parts along dimension 0, may hold values from -260 to 260
- tenant_ids: int32 [16, 256], P(('groups', 'dp')), parts along dimension 0, may hold values from 0 to 7, never falling along the last dimension, each value on 1 to 64 neighbouring positions
- cot_query: bfloat16 [4096, 4096], P(('groups', 'dp'), 'tensor'), parts along dimension 0, may hold values from -6 to 6
- cot_value: bfloat16 [4096, 1024], P(('groups', 'dp'), 'tensor'), parts along dimension 0, may hold values from -6 to 6
- w_query: bfloat16 [8192, 4096], P(None, 'tensor'), may hold values from -0.0625 to 0.0625
- w_value: bfloat16 [8192, 1024], P(None, 'tensor'), may hold values from -0.0625 to 0.0625
- a_query: bfloat16 [8, 64, 8192], P('dp', None, 'tensor'), may hold values from -0.0625 to 0.0625
- a_value: bfloat16 [8, 64, 8192], P('dp', None, 'tensor'), may hold values from -0.0625 to 0.0625
- b_query: bfloat16 [8, 64, 4096], P('dp', None, 'tensor'), may hold values from -0.09375 to 0.09375
- b_value: bfloat16 [8, 64, 1024], P('dp', None, 'tensor'), may hold values from -0.1875 to 0.1875
Outputs:
- input_grad: bfloat16 [4096, 8192], P(('groups', 'dp'), 'tensor'), parts along dimension 0
- grad_a_query: float32 [16, 64, 8192], P(('groups', 'dp'), None, 'tensor'), parts along dimension 0
- grad_a_value: float32 [16, 64, 8192], P(('groups', 'dp'), None, 'tensor'), parts along dimension 0
- grad_b_query: float32 [16, 64, 4096], P(('groups', 'dp'), None, 'tensor'), parts along dimension 0
- grad_b_value: float32 [16, 64, 1024], P(('groups', 'dp'), None, 'tensor'), parts along dimension 0
There are 2 independent parts, one for each index of `groups`. A program takes and returns all parts, laid end to end along the dimension named above; an argument that names none is the same for every part. Nothing has to cross between parts.
Inputs may be any that keep to these rules, and one draw needn't show every extreme that they name: `tenant_ids`: on each line of 256 rows the tenant ids never fall, every one of the 8 tenants holds 1 to 64 rows, and some tenant holds exactly 64.
All inputs are finite; a program needn't handle non-finite values.
Results may differ from a plain program's by a relative error of at most 0.017.
Values may be sent and summed in bfloat16 or wider, within the bound.
A program may use at most 192 MiB of HBM per device.

v0:
```python
import math

import jax
import jax.numpy as jnp
from jax import lax
from jax.sharding import PartitionSpec as P

D = 8192
QW = 4096
KV = 1024
R = 64


SCALE = 2.0
CLIP_RMS = 0.5


def contract_rows(left, right):
    return lax.dot_general(
        left, right, (((0,), (0,)), ((), ())), preferred_element_type=jnp.float32
    )


def contract_cols(left, right):
    return lax.dot_general(
        left, right, (((1,), (1,)), ((), ())), preferred_element_type=jnp.float32
    )


def on_device(
    tokens, tenant_ids, cot_query, cot_value, w_query, w_value, a_query, a_value, b_query, b_value
):
    tenant_row = tenant_ids[0]
    owned, rank_dim, feat_local = a_query.shape
    query_local = b_query.shape[2]
    all_aq, all_av, all_bq, all_bv = (
        lax.all_gather(a_query, "dp", axis=0, tiled=True),
        lax.all_gather(a_value, "dp", axis=0, tiled=True),
        lax.all_gather(b_query, "dp", axis=0, tiled=True),
        lax.all_gather(b_value, "dp", axis=0, tiled=True),
    )
    tenants = all_aq.shape[0]
    flat_aq = all_aq.reshape(tenants * rank_dim, feat_local)
    flat_av = all_av.reshape(tenants * rank_dim, feat_local)
    flat_bq = all_bq.reshape(tenants * rank_dim, query_local)
    flat_bv = all_bv.reshape(tenants * rank_dim, b_value.shape[2])
    part_hq = contract_cols(tokens, flat_aq)
    part_hv = contract_cols(tokens, flat_av)
    part_gq = contract_cols(cot_query, flat_bq)
    part_gv = contract_cols(cot_value, flat_bv)
    sum_hq, sum_hv, sum_gq, sum_gv = (
        lax.psum(part_hq.astype(jnp.bfloat16), "tensor").astype(jnp.float32),
        lax.psum(part_hv.astype(jnp.bfloat16), "tensor").astype(jnp.float32),
        lax.psum(part_gq.astype(jnp.bfloat16), "tensor").astype(jnp.float32),
        lax.psum(part_gv.astype(jnp.bfloat16), "tensor").astype(jnp.float32),
    )
    column_tenant = jnp.arange(tenants * rank_dim, dtype=jnp.int32) // rank_dim
    row_mask = (tenant_row[:, None] == column_tenant[None, :]).astype(jnp.float32)
    masked_hq = (sum_hq * row_mask).astype(jnp.bfloat16)
    masked_hv = (sum_hv * row_mask).astype(jnp.bfloat16)
    masked_gq = (sum_gq * row_mask).astype(jnp.bfloat16)
    masked_gv = (sum_gv * row_mask).astype(jnp.bfloat16)
    frozen_part = lax.psum_scatter(
        (contract_cols(w_query, cot_query) + contract_cols(w_value, cot_value)).astype(
            jnp.bfloat16
        ),
        "tensor",
        scatter_dimension=0,
        tiled=True,
    ).astype(jnp.float32)
    adapter_term = jnp.dot(masked_gq, flat_aq, preferred_element_type=jnp.float32) + jnp.dot(
        masked_gv, flat_av, preferred_element_type=jnp.float32
    )
    input_grad = (frozen_part.T + SCALE * adapter_term).astype(jnp.bfloat16)
    summed = lax.psum_scatter(
        jnp.concatenate(
            [
                contract_rows(masked_gq, tokens),
                contract_rows(masked_gv, tokens),
                contract_rows(masked_hq, cot_query),
                contract_rows(masked_hv, cot_value),
            ],
            axis=1,
        ).astype(jnp.bfloat16),
        "dp",
        scatter_dimension=0,
        tiled=True,
    ).astype(jnp.float32)
    raw_aq = summed[:, :feat_local].reshape(owned, rank_dim, feat_local)
    raw_av = summed[:, feat_local : 2 * feat_local].reshape(owned, rank_dim, feat_local)
    raw_bq = summed[:, 2 * feat_local : 2 * feat_local + query_local].reshape(
        owned, rank_dim, query_local
    )
    raw_bv = summed[:, 2 * feat_local + query_local :].reshape(owned, rank_dim, -1)
    raw_aq = SCALE * raw_aq
    raw_av = SCALE * raw_av
    raw_bq = SCALE * raw_bq
    raw_bv = SCALE * raw_bv
    local_sq = jnp.sum(raw_aq * raw_aq, axis=(1, 2)) + jnp.sum(raw_av * raw_av, axis=(1, 2))
    local_sq = (
        local_sq + jnp.sum(raw_bq * raw_bq, axis=(1, 2)) + jnp.sum(raw_bv * raw_bv, axis=(1, 2))
    )
    total_sq = lax.psum(local_sq, "tensor")
    entries = float(R * (2 * D + QW + KV))
    factor = jnp.minimum(1.0, CLIP_RMS * math.sqrt(entries) / jnp.sqrt(total_sq + 1e-06))[
        :, None, None
    ]
    return (input_grad, raw_aq * factor, raw_av * factor, raw_bq * factor, raw_bv * factor)


def solution(mesh):
    in_specs = (
        P(("groups", "dp"), "tensor"),
        P(("groups", "dp"), None),
        P(("groups", "dp"), "tensor"),
        P(("groups", "dp"), "tensor"),
        P(None, "tensor"),
        P(None, "tensor"),
        P("dp", None, "tensor"),
        P("dp", None, "tensor"),
        P("dp", None, "tensor"),
        P("dp", None, "tensor"),
    )
    out_specs = (
        P(("groups", "dp"), "tensor"),
        P(("groups", "dp"), None, "tensor"),
        P(("groups", "dp"), None, "tensor"),
        P(("groups", "dp"), None, "tensor"),
        P(("groups", "dp"), None, "tensor"),
    )
    return jax.shard_map(
        on_device, mesh=mesh, in_specs=in_specs, out_specs=out_specs, check_vma=False
    )
```

profile of v0, /device:TPU:16, one launch (start us, length us, event | category | flops | bytes accessed | tf_op | source)
XLA Modules:
  0.0 377.7 jit_solution(1344626156137623663)
XLA Ops:
  7.2 0.0 copy-start
  7.2 0.0 all-gather.4.cloned.1.call-start
  7.2 0.7 all-gather.4.cloned.1.call-update
  7.9 0.0 all-gather.8.cloned.1.call-start
  8.0 0.7 all-gather.8.cloned.1.call-update
  8.7 0.0 all-gather.6.cloned.1.call-start
  8.7 0.7 all-gather.6.cloned.1.call-update
  9.4 0.0 all-reduce.3.cloned.1.call-start
  9.4 14.1 %all_gather.14 = bf16[8,64,512]{2,1,0:T(8,128)(2,1)S(1)} all-gather(bf16[1,64,512]{2,1,0:T(8,128)(2,1)} %param.19), channel_id=1, replica_groups=mesh['groups'=2,'dp'=8,'tensor'=2] {'dp'}, dimensions={0}, use_global_device_ids=true | all-gather | bytes 589824 | tf_op jit(solution)/shard_map/all_gather | solution.py:40
  23.6 2.0 convolution_convert_fusion.6
  25.6 0.0 copy-start.5
  25.6 9.2 %fusion.30 = f32[8192,256]{1,0:T(8,128)} fusion(bf16[8192,512]{1,0:T(8,128)(2,1)} %param.15, bf16[256,512]{1,0:T(8,128)(2,1)} %param.13), kind=kOutput, calls=%fused_computation.51 | convolution fusion | flops 2147483648 | bytes 17039360 | tf_op jit(solution)/shard_map/dot_general | solution.py:25
  34.7 5.3 %all-gather.4.cloned.1.call-done = bf16[8,64,2048]{2,1,0:T(8,128)(2,1)} async-done(((bf16[1,64,2048]{2,1,0:T(8,128)(2,1)}), bf16[8,64,2048]{2,1,0:T(8,128)(2,1)}) %all-gather.4.cloned.1.call-update) | async-done | bytes 2097168 | tf_op jit(solution)/shard_map/all_gather | solution.py:39
  40.0 0.0 copy-done.5
  40.0 3.0 convolution_convert_fusion.7
  43.1 44.7 %all-gather.8.cloned.1.call-done = bf16[8,64,4096]{2,1,0:T(8,128)(2,1)} async-done(((bf16[1,64,4096]{2,1,0:T(8,128)(2,1)}), bf16[8,64,4096]{2,1,0:T(8,128)(2,1)}) %all-gather.8.cloned.1.call-update) | async-done | bytes 4194320 | tf_op jit(solution)/shard_map/all_gather | solution.py:38
  87.8 0.0 copy-done
  87.8 4.2 %convolution_convert_fusion.4 = bf16[256,512]{1,0:T(8,128)(2,1)} fusion(bf16[256,4096]{1,0:T(8,128)(2,1)S(1)} %copy-done, bf16[512,4096]{1,0:T(8,128)(2,1)} %bitcast.37), kind=kOutput, calls=%fused_computation.11 | convolution fusion | flops 1073872896 | bytes 6553600 | tf_op jit(solution)/shard_map/dot_general | solution.py:25
  91.9 43.3 %all-gather.6.cloned.1.call-done = bf16[8,64,4096]{2,1,0:T(8,128)(2,1)} async-done(((bf16[1,64,4096]{2,1,0:T(8,128)(2,1)}), bf16[8,64,4096]{2,1,0:T(8,128)(2,1)}) %all-gather.6.cloned.1.call-update) | async-done | bytes 4194320 | tf_op jit(solution)/shard_map/all_gather | solution.py:37
  135.3 4.2 %convolution_convert_fusion.5 = bf16[256,512]{1,0:T(8,128)(2,1)} fusion(bf16[256,4096]{1,0:T(8,128)(2,1)S(1)} %copy-done, bf16[512,4096]{1,0:T(8,128)(2,1)} %bitcast.35), kind=kOutput, calls=%fused_computation.12 | convolution fusion | flops 1073872896 | bytes 6553600 | tf_op jit(solution)/shard_map/dot_general | solution.py:25
  139.4 0.0 all-reduce.3.cloned.1.call-update
  139.5 0.0 reduce-scatter.3.cloned.1.call-start
  139.5 20.2 %fusion = bf16[8192,256]{1,0:T(8,128)(2,1)} fusion(f32[8192,256]{1,0:T(8,128)} %fusion.30, bf16[8192,2048]{1,0:T(8,128)(2,1)} %param.14, bf16[256,2048]{1,0:T(8,128)(2,1)S(1)} %copy-done.5), kind=kOutput, calls=%fused_computation.2 | convolution fusion | flops 8594128896 | bytes 47185920 | tf_op jit(solution)/shard_map/dot_general | solution.py:25
  159.7 0.0 copy-start.2
  159.7 0.0 copy-start.6
  159.7 0.0 reduce-scatter.3.cloned.1.call-update
  159.7 0.2 reduce-scatter.5.cloned.1.call-start
  159.9 20.4 %all-reduce.3.cloned.1.call-done = (bf16[256,512]{1,0:T(8,128)(2,1)}, bf16[256,512]{1,0:T(8,128)(2,1)}, bf16[256,512]{1,0:T(8,128)(2,1)}, bf16[256,512]{1,0:T(8,128)(2,1)}) async-done(((bf16[256,512]{1,0:T(8,128)(2,1)}, bf16[256,512]{1,0:T(8,128)(2,1)}, bf16[256,512]{1,0:T(8,128)(2,1)}, bf16[256,512]{1,0:T(8,128)(2,1)}), (bf16[256,512]{1,0:T(8,128)(2,1)}, bf16[256,512]{1,0:T(8,128)(2,1)}, ...) | async-done | bytes 1048592 | tf_op jit(solution)/shard_map/psum | solution.py:54
  180.3 0.0 copy-start.3
  180.3 0.0 copy-done.2
  180.3 0.0 copy-done.6
  180.3 1.4 convolution_convert_fusion.3
  181.7 0.0 copy-start.4
  181.7 2.2 convolution_convert_fusion.2
  183.9 0.0 copy-done.3
  183.9 1.4 convolution_convert_fusion
  185.3 0.0 copy-done.4
  185.3 1.4 convolution_convert_fusion.1
  186.7 6.8 %pad_maximum_fusion = bf16[512,10752]{1,0:T(8,128)(2,1)} fusion(bf16[512,512]{1,0:T(8,128)(2,1)S(1)} %convolution_convert_fusion.3, bf16[512,2048]{1,0:T(8,128)(2,1)S(1)} %convolution_convert_fusion.2, bf16[512,4096]{1,0:T(8,128)(2,1)S(1)} %convolution_convert_fusion, bf16[512,4096]{1,0:T(8,128)(2,1)S(1)} %convolution_convert_fusion.1), kind=kLoop, calls=%fused_computation | loop fusion | flops 44040192 | bytes 22020096 | tf_op jit(solution)/shard_map/concatenate | solution.py:76
  193.4 0.0 reduce-scatter.5.cloned.1.call-update
  193.5 6.1 %fusion.19 = f32[256,4096]{0,1:T(8,128)} fusion(bf16[512,4096]{1,0:T(8,128)(2,1)} %bitcast.36, bf16[256,512]{1,0:T(8,128)(2,1)S(1)} %copy-done.4, s32[512]{0:T(512)S(1)} %add_select_fusion, s32[256]{0:T(256)S(1)} %bitcast.44), kind=kOutput, calls=%fused_computation.37 | convolution fusion | flops 1074266112 | bytes 8653824 | tf_op jit(solution)/shard_map/dot_general | solution.py:71
  199.5 37.4 %reduce-scatter.3.cloned.1.call-done = bf16[4096,256]{1,0:T(8,128)(2,1)} async-done(((bf16[8192,256]{1,0:T(8,128)(2,1)}), bf16[4096,256]{1,0:T(8,128)(2,1)}) %reduce-scatter.3.cloned.1.call-update) | async-done | bytes 2097168 | tf_op jit(solution)/shard_map/reduce_scatter | solution.py:63
  236.9 7.4 %fusion.3 = bf16[256,4096]{0,1:T(8,128)(2,1)} fusion(f32[256,4096]{0,1:T(8,128)} %fusion.19, bf16[512,4096]{1,0:T(8,128)(2,1)} %bitcast.38, bf16[4096,256]{1,0:T(8,128)(2,1)} %reduce-scatter.3.cloned.1.call-done, bf16[256,512]{1,0:T(8,128)(2,1)S(1)} %copy-done.3, s32[512]{0:T(512)S(1)} %add_select_fusion, s32[256]{0:T(256)S(1)} %bitcast.45), kind=kOutput, calls=%fused_computation.8 | convolution fusion | flops 1079508992 | bytes 12848128 | tf_op jit(solution)/shard_map/dot_general | solution.py:71
  244.3 4.2 %copy.22 = bf16[256,4096]{1,0:T(8,128)(2,1)} copy(bf16[256,4096]{0,1:T(8,128)(2,1)} %fusion.3) | data formatting | bytes 4194304
  248.4 102.5 %reduce-scatter.5.cloned.1.call-done = bf16[64,10752]{1,0:T(8,128)(2,1)} async-done(((bf16[512,10752]{1,0:T(8,128)(2,1)}), bf16[64,10752]{1,0:T(8,128)(2,1)}) %reduce-scatter.5.cloned.1.call-update) | async-done | bytes 1376272 | tf_op jit(solution)/shard_map/reduce_scatter | solution.py:75
  350.9 1.5 convert_element_type.62
  352.4 0.0 copy-start.1
  352.4 1.2 multiply_reduce_fusion
  353.6 0.7 multiply_reduce_fusion.2
  354.3 0.0 copy-done.1
  354.3 0.6 multiply_reduce_fusion.3
  357.5 6.1 %psum.39 = f32[1]{0:T(128)} all-reduce(f32[1]{0:T(128)} %bitcast.6), channel_id=1, replica_groups=mesh['groups'=2,'dp'=8,'tensor'=2] {'tensor'}, use_global_device_ids=true, to_apply=%region_10.11 | all-reduce | flops 1 | bytes 8 | tf_op jit(solution)/shard_map/psum | solution.py:103
  364.3 3.1 multiply_bitcast_fusion
  367.4 1.9 multiply_bitcast_fusion.2
  369.2 1.6 multiply_bitcast_fusion.3
  (1 shorter events, 0.0 us)
Async XLA Ops:
  7.2 80.6 %copy-start = (bf16[256,4096]{1,0:T(8,128)(2,1)S(1)}, bf16[256,4096]{1,0:T(8,128)(2,1)}, u32[]{:S(2)}) copy-start(bf16[256,4096]{1,0:T(8,128)(2,1)} %param.10) | copy-start | bytes 6291460
  7.2 32.8 %all-gather.4.cloned.1.call-start = ((), (), s32[]{:S(2)}) async-start(), calls=%async_computation.3 | async-start | bytes 2359296 | tf_op jit(solution)/shard_map/all_gather | solution.py:39
  7.9 79.8 %all-gather.8.cloned.1.call-start = ((), (), s32[]{:S(2)}) async-start(), calls=%async_computation.5 | async-start | bytes 4718592 | tf_op jit(solution)/shard_map/all_gather | solution.py:38
  8.7 126.6 %all-gather.6.cloned.1.call-start = ((), (), s32[]{:S(2)}) async-start(), calls=%async_computation.4 | async-start | bytes 4718592 | tf_op jit(solution)/shard_map/all_gather | solution.py:37
  9.4 170.9 %all-reduce.3.cloned.1.call-start = ((), (), s32[]{:S(2)}) async-start(), calls=%async_computation.7 | async-start | bytes 2097152 | tf_op jit(solution)/shard_map/psum | solution.py:54
  25.6 14.5 %copy-start.5 = (bf16[256,2048]{1,0:T(8,128)(2,1)S(1)}, bf16[256,2048]{1,0:T(8,128)(2,1)}, u32[]{:S(2)}) copy-start(bf16[256,2048]{1,0:T(8,128)(2,1)} %param.12) | copy-start | bytes 3145732
  139.5 97.4 %reduce-scatter.3.cloned.1.call-start = ((), (), s32[]{:S(2)}) async-start(), calls=%async_computation.2 | async-start | bytes 6291456 | tf_op jit(solution)/shard_map/reduce_scatter | solution.py:63
  159.7 20.6 %copy-start.2 = (bf16[256,512]{1,0:T(8,128)(2,1)S(1)}, bf16[256,512]{1,0:T(8,128)(2,1)}, u32[]{:S(2)}) copy-start(bf16[256,512]{1,0:T(8,128)(2,1)} %param.13) | copy-start | bytes 786436
  159.7 20.6 %copy-start.6 = (s32[1,256]{1,0:T(1,128)S(1)}, s32[1,256]{1,0:T(1,128)}, u32[]{:S(2)}) copy-start(s32[1,256]{1,0:T(1,128)} %param.11) | copy-start | bytes 3076
  159.7 191.2 %reduce-scatter.5.cloned.1.call-start = ((), (), s32[]{:S(2)}) async-start(), calls=%async_computation.6 | async-start | bytes 12386304 | tf_op jit(solution)/shard_map/reduce_scatter | solution.py:75
  180.3 3.6 copy-start.3
  181.7 3.6 copy-start.4
  352.4 1.9 copy-start.1
Sparse Core Ops, SparseCore 0:
  9.6 30.3 all-gather.3
  41.6 46.0 all-gather.7
  89.4 45.8 all-gather.5
  139.6 40.6 all-reduce.2
  182.6 54.3 reduce-scatter.2
  239.1 111.7 reduce-scatter.4
where the time goes:
time: 382 us; the launch traced here: 378 us
  waiting for transfers between devices  256 us (67%)
  matrix products  62.4 us (16%)
  blocking collectives  20.2 us (5%)
  between operations  17.5 us (5%)
  other arithmetic  17.3 us (5%)
  local copies, waits for them, and re-layouts  4.2 us (1%)
    reduce_scatter x1, waiting for transfers between devices, on_device(): lax.psum_scatter(jnp.concatenate([contract_rows(masked_gq, tokens), contr...  102 us
    all_gather x1, waiting for transfers between devices, on_device(): lax.all_gather(a_value, 'dp', axis=0, tiled=True)  44.7 us
    all_gather x1, waiting for transfers between devices, on_device(): lax.all_gather(a_query, 'dp', axis=0, tiled=True)  43.3 us
    dot_general x6, matrix products, contract_cols(): lax.dot_general(left, right, (((1,), (1,)), ((), ())), preferred_element_...  42.7 us
    reduce_scatter x1, waiting for transfers between devices, on_device(): lax.psum_scatter((contract_cols(w_query, cot_query) + contract_cols(w_val...  37.4 us
    psum x1, waiting for transfers between devices, on_device(): lax.psum(part_gq.astype(jnp.bfloat16), 'tensor').astype(jnp.float32)  20.4 us
    all_gather x1, blocking collectives, on_device(): lax.all_gather(b_value, 'dp', axis=0, tiled=True)  14.1 us
  transfers between devices with their start and end apart: 6, of which 6 were waited for; matrix products, arithmetic and copies ran while one was open for 18% of the time, Pallas kernels for 0%

commit v1 on v0

v1 whole, which is shorter than its diff:
```python
import functools
import math

import jax
import jax.numpy as jnp
from jax import lax
from jax.experimental import pallas as pl
from jax.experimental.pallas import tpu as pltpu
from jax.sharding import PartitionSpec as P

D = 8192
QW = 4096
KV = 1024
R = 64

SCALE = 2.0
CLIP_RMS = 0.5
MESH = pl.DeviceIdType.MESH
PIECE = 16


def dot_cols(left, right):
    return lax.dot_general(
        left, right, (((1,), (1,)), ((), ())), preferred_element_type=jnp.float32
    )


def remote(src, dst, send, recv, where):
    return pltpu.make_async_remote_copy(
        src_ref=src, dst_ref=dst, send_sem=send, recv_sem=recv, device_id=where, device_id_type=MESH
    )


def greet(z, nz, pairs, t, nt, x_partner):
    barrier = pltpu.get_barrier_semaphore()

    def signal(where):
        pl.semaphore_signal(barrier, inc=1, device_id=where, device_id_type=MESH)

    left, right, core = pairs

    @pl.when(z > 0)
    def _():
        signal({"dp": left})

    @pl.when(z < nz - 1)
    def _():
        signal({"dp": right})

    signal({"dp": core})
    if x_partner is not None:
        signal({"groups": x_partner})
    for d in range(nt - 1):
        signal({"tensor": lax.rem(t + 1 + d, nt)})
    always = 1 + (x_partner is not None) + nt - 1
    ends = jnp.where(z > 0, 1, 0) + jnp.where(z < nz - 1, 1, 0)
    pl.semaphore_wait(barrier, always + ends)


def gather_kernel(
    n_dp, nt, tile,
    mine, cq, cv, wq, wv,
    full, frozen, parts,
    wq_buf, wv_buf, out_buf,
    w_sem, l_sem, own_send, own_recv, z_send, z_recv, x_send, x_recv, c_send, c_recv,
    p_send, p_recv,
):
    nz = n_dp // 2
    me = lax.axis_index("dp")
    g = lax.axis_index("groups")
    t = lax.axis_index("tensor")
    z, c = me // 2, lax.rem(me, 2)
    other = 1 - g
    core = 2 * z + 1 - c
    left, right = me - 2, me + 2
    half = R // 2
    npiece = half // PIECE

    def rows(which, p):
        return pl.ds(pl.multiple_of(which * half + p * PIECE, PIECE), PIECE)

    def tiles(i, slot):
        per = frozen.shape[1] // tile
        peer = lax.rem(t + 1 + i // per, nt)
        at = pl.ds(pl.multiple_of(peer * frozen.shape[1] + lax.rem(i, per) * tile, tile), tile)
        return (
            pltpu.make_async_copy(wq.at[at], wq_buf.at[slot], w_sem.at[0, slot]),
            pltpu.make_async_copy(wv.at[at], wv_buf.at[slot], w_sem.at[1, slot]),
        )

    for copy in tiles(0, 0):
        copy.start()

    greet(z, nz, (left, right, core), t, nt, other)

    def z_copy(way, k, p, source):
        slot = 2 * (z - k if way == 0 else z + k) + c
        at = rows(g, p)
        src = mine.at[at] if source else full.at[slot, at]
        return remote(
            src, full.at[slot, at], z_send.at[way, k, p], z_recv.at[way, k, p],
            {"dp": right if way == 0 else left},
        )

    def z_arrival(way, k, p):
        slot = 2 * (z - k - 1 if way == 0 else z + k + 1) + c
        at = full.at[slot, rows(g, p)]
        return remote(
            at, at, z_send.at[way, k, p], z_recv.at[way, k, p],
            {"dp": right if way == 0 else left},
        )

    def x_copy(way, k, p, arriving):
        slot = 2 * (z - k - 1 if way == 0 else z + k + 1) + c
        at = full.at[slot, rows(other if arriving else g, p)]
        return remote(at, at, x_send.at[way, k, p], x_recv.at[way, k, p], {"groups": other})

    def c_copy(which, way, k, p, arriving):
        slot = 2 * (z - k - 1 if way == 0 else z + k + 1) + (1 - c if arriving else c)
        at = full.at[slot, rows(g if which == 0 else other, p)]
        return remote(
            at, at, c_send.at[which, way, k, p], c_recv.at[which, way, k, p], {"dp": core}
        )

    def sends(way, k):
        if way == 0:
            return jnp.logical_and(z - k >= 0, z < nz - 1)
        return jnp.logical_and(z + k <= nz - 1, z > 0)

    def gets(way, k):
        return z - k - 1 >= 0 if way == 0 else z + k + 1 <= nz - 1

    for p in range(npiece):
        for way in range(2):
            @pl.when(sends(way, 0))
            def _(way=way, p=p):
                z_copy(way, 0, p, True).start()

    local = pltpu.make_async_copy(mine, full.at[me], l_sem)
    local.start()
    own = remote(mine, full.at[me], own_send, own_recv, {"dp": core})
    own.start()
    own_in = remote(mine, full.at[core], own_send, own_recv, {"dp": core})

    per = frozen.shape[1] // tile
    total, away = nt * per, (nt - 1) * per

    def p_copy(i):
        at = pl.ds(pl.multiple_of(lax.rem(i, per) * tile, tile), tile)
        peer = lax.rem(t + 1 + i // per, nt)
        return remote(
            out_buf.at[i], parts.at[i // per, :, at], p_send.at[i], p_recv.at[i], {"tensor": peer}
        )

    def step(i, carry):
        slot = lax.rem(i, 2)
        for copy in tiles(i, slot):
            copy.wait()

        @pl.when(i + 1 < total)
        def _():
            for copy in tiles(i + 1, 1 - slot):
                copy.start()

        value = dot_cols(cq[...], wq_buf[slot]) + dot_cols(cv[...], wv_buf[slot])
        value = value.astype(jnp.bfloat16)

        @pl.when(i < away)
        def _():
            out_buf[i] = value
            p_copy(i).start()

        @pl.when(i >= away)
        def _():
            at = pl.ds(pl.multiple_of(lax.rem(i, per) * tile, tile), tile)
            frozen[:, at] = value

        return carry

    lax.fori_loop(0, total, step, 0)

    def from_x(k):
        for p in range(npiece):
            for way in range(2):
                @pl.when(gets(way, k))
                def _(way=way, p=p):
                    x_copy(way, k, p, True).wait_recv()
                    c_copy(1, way, k, p, False).start()

    for k in range(nz - 1):
        for p in range(npiece):
            for way in range(2):
                @pl.when(gets(way, k))
                def _(way=way, p=p, k=k):
                    z_arrival(way, k, p).wait_recv()
                    if k + 1 < nz - 1:
                        @pl.when(sends(way, k + 1))
                        def _():
                            z_copy(way, k + 1, p, False).start()
                    x_copy(way, k, p, False).start()
                    c_copy(0, way, k, p, False).start()
        if k > 0:
            from_x(k - 1)
    from_x(nz - 2)

    own_in.wait_recv()
    for k in range(nz - 1):
        for p in range(npiece):
            for way in range(2):
                @pl.when(gets(way, k))
                def _(way=way, p=p, k=k):
                    for which in range(2):
                        c_copy(which, way, k, p, True).wait_recv()
                        c_copy(which, way, k, p, False).wait_send()
                    x_copy(way, k, p, False).wait_send()

                @pl.when(sends(way, k))
                def _(way=way, p=p, k=k):
                    z_copy(way, k, p, k == 0).wait_send()
    own.wait_send()
    local.wait()

    def finish(i, carry):
        p_copy(i).wait_recv()
        p_copy(i).wait_send()
        return carry

    lax.fori_loop(0, away, finish, 0)


def gather(mine, cq, cv, wq, wv, n_dp, nt):
    rank, width = mine.shape
    rows = cq.shape[0]
    feat = wq.shape[0] // nt
    tile = min(512, feat)
    nz = n_dp // 2
    npiece = R // 2 // PIECE
    away = (nt - 1) * (feat // tile)
    bf = jnp.bfloat16
    hbm = pl.BlockSpec(memory_space=pl.ANY)
    vmem = pl.BlockSpec(memory_space=pltpu.VMEM)
    dma = pltpu.SemaphoreType.DMA
    return pl.pallas_call(
        functools.partial(gather_kernel, n_dp, nt, tile),
        out_shape=(
            jax.ShapeDtypeStruct((n_dp, rank, width), bf),
            jax.ShapeDtypeStruct((rows, feat), bf),
            jax.ShapeDtypeStruct((nt - 1, rows, feat), bf),
        ),
        in_specs=[hbm, vmem, vmem, hbm, hbm],
        out_specs=(hbm, vmem, hbm),
        scratch_shapes=[
            pltpu.VMEM((2, tile, wq.shape[1]), bf),
            pltpu.VMEM((2, tile, wv.shape[1]), bf),
            pltpu.VMEM((away, rows, tile), bf),
            dma((2, 2)),
            dma,
            dma,
            dma,
            dma((2, nz - 1, npiece)),
            dma((2, nz - 1, npiece)),
            dma((2, nz - 1, npiece)),
            dma((2, nz - 1, npiece)),
            dma((2, 2, nz - 1, npiece)),
            dma((2, 2, nz - 1, npiece)),
            dma((away,)),
            dma((away,)),
        ],
        compiler_params=pltpu.CompilerParams(
            collective_id=0, has_side_effects=True, vmem_limit_bytes=40 * 2**20
        ),
    )(mine, cq, cv, wq, wv)


def grads_kernel(
    n_dp, nt, col,
    ranks, ids, tokens, cq, cv,
    aq, av, bq, bv,
    own, from_core, from_z, sq_out, sq_in,
    core_send, core_recv, z_send, z_recv, n_send, n_recv,
):
    nz = n_dp // 2
    me = lax.axis_index("dp")
    t = lax.axis_index("tensor")
    z, c = me // 2, lax.rem(me, 2)
    core = 2 * z + 1 - c
    left, right = me - 2, me + 2
    feat, query, value = tokens.shape[1], cq.shape[1], cv.shape[1]
    npiece = R // PIECE
    f32, bf = jnp.float32, jnp.bfloat16

    greet(z, nz, (left, right, core), t, nt, None)

    def contribute(tenant):
        masked = jnp.where(ids[...] == tenant, ranks[...].astype(f32), 0.0).astype(bf)
        to_a, to_bq, to_bv = masked[: 2 * R], masked[2 * R : 3 * R], masked[3 * R :]

        def over(width, body):
            step = min(col, width)

            def run(i, carry):
                body(pl.multiple_of(i * step, step), step)
                return carry

            lax.fori_loop(0, width // step, run, 0)

        def a_part(at, step):
            got = jnp.dot(to_a, tokens[:, pl.ds(at, step)], preferred_element_type=f32).astype(bf)
            own[tenant, :, pl.ds(at, step)] = got[:R]
            own[tenant, :, pl.ds(pl.multiple_of(feat + at, 128), step)] = got[R:]

        def bq_part(at, step):
            got = jnp.dot(to_bq, cq[:, pl.ds(at, step)], preferred_element_type=f32).astype(bf)
            own[tenant, :, pl.ds(pl.multiple_of(2 * feat + at, 128), step)] = got

        def bv_part(at, step):
            got = jnp.dot(to_bv, cv[:, pl.ds(at, step)], preferred_element_type=f32).astype(bf)
            own[tenant, :, pl.ds(pl.multiple_of(2 * feat + query + at, 128), step)] = got

        over(feat, a_part)
        over(query, bq_part)
        over(value, bv_part)

    def core_copy(zt):
        return remote(
            own.at[2 * zt + 1 - c], from_core.at[zt], core_send.at[zt], core_recv.at[zt],
            {"dp": core},
        )

    def pair_sum(zt):
        core_copy(zt).wait_recv()
        own[2 * zt + c] = (own[2 * zt + c].astype(f32) + from_core[zt].astype(f32)).astype(bf)

    def z_copy(way, zt, p):
        at = pl.ds(p * PIECE, PIECE)
        return remote(
            own.at[2 * zt + c, at], from_z.at[way, zt, at], z_send.at[way, zt, p],
            z_recv.at[way, zt, p], {"dp": right if way == 0 else left},
        )

    def target(way, tau):
        return nz - 1 - (tau - z) if way == 0 else tau - (nz - 1 - z)

    def active(way, tau):
        return tau >= z if way == 0 else tau >= nz - 1 - z

    def pass_on(way, tau, p):
        zt = target(way, tau)

        @pl.when(active(way, tau))
        def _():
            at = pl.ds(p * PIECE, PIECE)

            @pl.when(z > 0 if way == 0 else z < nz - 1)
            def _():
                z_copy(way, zt, p).wait_recv()
                own[2 * zt + c, at] = (
                    own[2 * zt + c, at].astype(f32) + from_z[way, zt, at].astype(f32)
                ).astype(bf)

            z_copy(way, zt, p).start()

    def sent(way, tau, p):
        @pl.when(active(way, tau))
        def _():
            z_copy(way, target(way, tau), p).wait_send()

    order = []
    for j in range((nz + 1) // 2):
        order += [nz - 1 - j] + ([j] if j != nz - 1 - j else [])

    for n, zt in enumerate(order):
        contribute(2 * zt + 1 - c)
        core_copy(zt).start()
        contribute(2 * zt + c)
        if n == 1:
            for earlier in order[:2]:
                pair_sum(earlier)
            for p in range(npiece):
                for way in range(2):
                    @pl.when(z == 0 if way == 0 else z == nz - 1)
                    def _(way=way, p=p):
                        pass_on(way, 0, p)
        elif n > 1:
            pair_sum(zt)

    for tau in range(1, nz - 1):
        for p in range(npiece):
            for way in range(2):
                sent(way, tau - 1, p)
                pass_on(way, tau, p)

    total = jnp.zeros((1, 1), f32)
    places = ((aq, 0, feat), (av, feat, feat), (bq, 2 * feat, query), (bv, 2 * feat + query, value))
    for p in range(npiece):
        at = pl.ds(p * PIECE, PIECE)
        for way in range(2):
            @pl.when(z > 0 if way == 0 else z < nz - 1)
            def _(way=way):
                z_copy(way, z, p).wait_recv()

        have_left, have_right = z > 0, z < nz - 1
        for ref, first, width in places:
            cols = pl.ds(first, width)
            sums = own[me, at, cols].astype(f32)
            ref[at, :] = sums

            @pl.when(have_left)
            def _(ref=ref, cols=cols):
                ref[at, :] += from_z[0, z, at, cols].astype(f32)

            @pl.when(have_right)
            def _(ref=ref, cols=cols):
                ref[at, :] += from_z[1, z, at, cols].astype(f32)

            sums = SCALE * ref[at, :]
            ref[at, :] = sums
            total = total + jnp.sum(sums * sums, axis=(0, 1), keepdims=True)

    sq_out[...] = jnp.broadcast_to(total, sq_out.shape)

    def n_copy(d):
        return remote(
            sq_out, sq_in.at[d], n_send.at[d], n_recv.at[d], {"tensor": lax.rem(t + 1 + d, nt)}
        )

    for d in range(nt - 1):
        n_copy(d).start()
    norm = sq_out[0:1, 0:1]
    for d in range(nt - 1):
        n_copy(d).wait_recv()
        norm = norm + sq_in[d, 0:1, 0:1]
    entries = float(R * (2 * D + QW + KV))
    factor = jnp.minimum(1.0, CLIP_RMS * math.sqrt(entries) / jnp.sqrt(norm + 1e-06))
    for ref, _, _ in places:
        ref[...] = ref[...] * factor

    for d in range(nt - 1):
        n_copy(d).wait_send()
    for zt in range(nz):
        core_copy(zt).wait_send()
    for p in range(npiece):
        for way in range(2):
            sent(way, nz - 2, p)


def grads(ranks, ids, tokens, cq, cv, n_dp, nt):
    feat, query, value = tokens.shape[1], cq.shape[1], cv.shape[1]
    width = 2 * feat + query + value
    nz = n_dp // 2
    npiece = R // PIECE
    bf, f32 = jnp.bfloat16, jnp.float32
    vmem = pl.BlockSpec(memory_space=pltpu.VMEM)
    dma = pltpu.SemaphoreType.DMA
    return pl.pallas_call(
        functools.partial(grads_kernel, n_dp, nt, 1024),
        out_shape=tuple(jax.ShapeDtypeStruct((R, w), f32) for w in (feat, feat, query, value)),
        in_specs=[vmem] * 5,
        out_specs=(vmem,) * 4,
        scratch_shapes=[
            pltpu.VMEM((n_dp, R, width), bf),
            pltpu.VMEM((nz, R, width), bf),
            pltpu.VMEM((2, nz, R, width), bf),
            pltpu.VMEM((8, 128), f32),
            pltpu.VMEM((nt - 1, 8, 128), f32),
            dma((nz,)),
            dma((nz,)),
            dma((2, nz, npiece)),
            dma((2, nz, npiece)),
            dma((nt - 1,)),
            dma((nt - 1,)),
        ],
        compiler_params=pltpu.CompilerParams(
            collective_id=1, has_side_effects=True, vmem_limit_bytes=52 * 2**20
        ),
    )(ranks, ids, tokens, cq, cv)


def on_device(
    n_dp, nt,
    tokens, tenant_ids, cot_query, cot_value, w_query, w_value, a_query, a_value, b_query, b_value
):
    bf, f32 = jnp.bfloat16, jnp.float32
    feat, query = a_query.shape[2], b_query.shape[2]
    rows = tokens.shape[0]
    mine = jnp.concatenate([a_query[0], a_value[0], b_query[0], b_value[0]], axis=1)
    full, frozen, parts = gather(mine, cot_query, cot_value, w_query, w_value, n_dp, nt)
    flat = full.reshape(n_dp * R, full.shape[2])
    flat_aq, flat_av = flat[:, :feat], flat[:, feat : 2 * feat]
    flat_bq, flat_bv = flat[:, 2 * feat : 2 * feat + query], flat[:, 2 * feat + query :]
    mask = tenant_ids[0][:, None] == jnp.arange(n_dp, dtype=jnp.int32)[None, :]

    def pick(part):
        part = part.reshape(rows, n_dp, R)
        return jnp.sum(jnp.where(mask[:, :, None], part, 0.0), axis=1)

    part = jnp.concatenate(
        [
            pick(dot_cols(cot_query, flat_bq)),
            pick(dot_cols(cot_value, flat_bv)),
            pick(dot_cols(tokens, flat_aq)),
            pick(dot_cols(tokens, flat_av)),
        ],
        axis=1,
    ).astype(bf)
    if nt == 2:
        got = lax.ppermute(part, "tensor", [(0, 1), (1, 0)])
        ranks = (part.astype(f32) + got.astype(f32)).astype(bf)
    else:
        ranks = lax.psum(part, "tensor")

    def spread(own):
        return jnp.where(mask[:, :, None], own[:, None, :], 0).reshape(rows, n_dp * R)

    adapter = jnp.dot(spread(ranks[:, :R]), flat_aq, preferred_element_type=f32) + jnp.dot(
        spread(ranks[:, R : 2 * R]), flat_av, preferred_element_type=f32
    )
    total = frozen.astype(f32)
    for d in range(nt - 1):
        total = total + parts[d].astype(f32)
    input_grad = (total + SCALE * adapter).astype(bf)
    outs = grads(ranks.T, tenant_ids, tokens, cot_query, cot_value, n_dp, nt)
    return (input_grad,) + tuple(out[None] for out in outs)


def solution(mesh):
    n_dp, nt = mesh.shape["dp"], mesh.shape["tensor"]
    in_specs = (
        P(("groups", "dp"), "tensor"),
        P(("groups", "dp"), None),
        P(("groups", "dp"), "tensor"),
        P(("groups", "dp"), "tensor"),
        P(None, "tensor"),
        P(None, "tensor"),
        P("dp", None, "tensor"),
        P("dp", None, "tensor"),
        P("dp", None, "tensor"),
        P("dp", None, "tensor"),
    )
    out_specs = (
        P(("groups", "dp"), "tensor"),
        P(("groups", "dp"), None, "tensor"),
        P(("groups", "dp"), None, "tensor"),
        P(("groups", "dp"), None, "tensor"),
        P(("groups", "dp"), None, "tensor"),
    )
    return jax.shard_map(
        functools.partial(on_device, n_dp, nt),
        mesh=mesh, in_specs=in_specs, out_specs=out_specs, check_vma=False,
    )
```

time: 382 us -> 214 us (0.56); the launches traced: 378 us -> 214 us
  waiting for transfers between devices: 256 us -> 4.24 us
  Pallas kernels: 0 us -> 185 us
  matrix products: 62.4 us -> 14.3 us
  blocking collectives: 20.2 us -> 0 us
  between operations: 17.5 us -> 0.8 us
  other arithmetic: 17.3 us -> 1.71 us
    pallas_call x0 -> x2, Pallas kernels: none -> 185 us  [the longest x1 108 us: grads(): pl.pallas_call(functools.partial(grads_kernel, n_dp, nt, 1024), out_shape...]
    reduce_scatter x2 -> x0, waiting for transfers between devices: 140 us -> none  [the longest x1 102 us: on_device(): lax.psum_scatter(jnp.concatenate([contract_rows(masked_gq, tokens), contr...]
    all_gather x3 -> x0, waiting for transfers between devices: 93.3 us -> none  [the longest x1 44.7 us: on_device(): lax.all_gather(a_value, 'dp', axis=0, tiled=True)]
    dot_general x12 -> x6, matrix products: 62.4 us -> 14.3 us  [the longest x4 7.37 us: dot_cols(): lax.dot_general(left, right, (((1,), (1,)), ((), ())), preferred_element_...]
    psum x1 -> x0, waiting for transfers between devices: 20.4 us -> none  [on_device(): lax.psum(part_gq.astype(jnp.bfloat16), 'tensor').astype(jnp.float32)]
    all_gather x1 -> x0, blocking collectives: 14.1 us -> none  [on_device(): lax.all_gather(b_value, 'dp', axis=0, tiled=True)]
    mul x3 -> x0, other arithmetic: 6.5 us -> none  [the longest x1 3.05 us: on_device(): raw_av * factor]
    psum x1 -> x0, blocking collectives: 6.06 us -> none  [on_device(): total_sq = lax.psum(local_sq, 'tensor')]
  transfers between devices with their start and end apart: 6 -> 1, of which waited for: 6 -> 1; matrix products, arithmetic and copies ran while one was open for 18% -> 0% of each run, Pallas kernels for 0% -> 0%
where the time goes in v1:
time: 214 us
  Pallas kernels  185 us (86%)
  matrix products  14.3 us (7%)
  local copies, waits for them, and re-layouts  5.75 us (3%)
  waiting for transfers between devices  4.24 us (2%)
    pallas_call x1, Pallas kernels, grads(): pl.pallas_call(functools.partial(grads_kernel, n_dp, nt, 1024), out_shape...  108 us
    pallas_call x1, Pallas kernels, gather(): pl.pallas_call(functools.partial(gather_kernel, n_dp, nt, tile), out_shap...  77.4 us
    dot_general x4, matrix products, dot_cols(): lax.dot_general(left, right, (((1,), (1,)), ((), ())), preferred_element_...  7.37 us
    unnamed x20, local copies, waits for them, and re-layouts  5.74 us
    dot_general x1, matrix products, on_device(): jnp.dot(spread(ranks[:, R:2 * R]), flat_av, preferred_element_type=f32)  5.64 us
  transfers between devices with their start and end apart: 1, of which 1 were waited for; matrix products, arithmetic and copies ran while one was open for 0% of the time, Pallas kernels for 0%

profile of v1, /device:TPU:16, one launch (start us, length us, event | category | flops | bytes accessed | tf_op | source)
XLA Modules:
  0.0 213.5 jit_solution(12848567616354644236)
XLA Ops:
  0.6 1.4 pad_maximum_fusion.mine
  2.0 0.0 copy-start
  2.1 1.2 copy-done
  3.3 0.0 copy-start.1
  3.3 0.9 copy-done.1
  4.2 0.0 copy-start.5
  4.2 77.4 %shard_map.137 = (bf16[8,64,10752]{2,1,0:T(8,128)(2,1)}, bf16[256,4096]{1,0:T(8,128)(2,1)S(1)}, bf16[1,256,4096]{2,1,0:T(8,128)(2,1)S(1)}) custom-call(bf16[64,10752]{1,0:T(8,128)(2,1)S(1)} %pad_maximum_fusion.mine, bf16[256,2048]{1,0:T(8,128)(2,1)S(1)} %copy-done, bf16[256,512]{1,0:T(8,128)(2,1)S(1)} %copy-done.1, bf16[8192,2048]{1,0:T(8,128)(2,1)} %wq.1, ...), custom_call_target="tpu_custom_call" | custom-call | tf_op jit(solution)/shard_map/pallas_call | solution.py:243
  81.6 0.0 copy-start.4
  81.6 1.5 fusion.12
  83.1 0.0 copy-done.5
  83.2 3.8 %fusion.8 = f32[512,256]{1,0:T(8,128)S(1)} fusion(bf16[256,4096]{1,0:T(8,128)(2,1)S(1)} %copy-done.5, bf16[512,10752]{1,0:T(8,128)(2,1)} %bitcast.39), kind=kOutput, calls=%fused_computation.10 | convolution fusion | flops 1073741824 | bytes 6815744 | tf_op jit(solution)/shard_map/dot_general | solution.py:23
  87.0 0.2 copy-done.4
  87.2 1.3 fusion.4
  88.5 0.0 copy-start.3
  88.5 0.7 fusion.10
  89.2 0.0 copy-done.3
  89.2 0.2 select_reduce_fusion.3
  89.5 1.6 collective-permute-start
  91.1 4.2 %collective-permute-done = bf16[256,256]{0,1:T(8,128)(2,1)S(1)} collective-permute-done((bf16[256,256]{0,1:T(8,128)(2,1)S(1)}, bf16[256,256]{0,1:T(8,128)(2,1)S(1)}, u32[]{:S(2)}, u32[]{:S(2)}) %collective-permute-start) | collective-permute-done | bytes 131104 | tf_op jit(solution)/shard_map/ppermute | solution.py:507
  95.4 0.0 copy-start.2
  95.4 1.3 fusion.6
  96.7 0.0 copy-done.2
  96.7 107.7 %shard_map.138 = (f32[64,4096]{1,0:T(8,128)}, f32[64,4096]{1,0:T(8,128)}, f32[64,2048]{1,0:T(8,128)S(1)}, f32[64,512]{1,0:T(8,128)S(1)}) custom-call(bf16[256,256]{1,0:T(8,128)(2,1)S(1)} %bitcast.34, s32[1,256]{1,0:T(1,128)S(1)} %copy-done.3, bf16[256,4096]{1,0:T(8,128)(2,1)} %tokens.1, bf16[256,2048]{1,0:T(8,128)(2,1)} %cq.3, bf16[256,512]{1,0:T(8,128)(2,1)S(1)} %copy-done.2), custom_call_target="tpu_custom_call" | custom-call | tf_op jit(solution)/shard_map/pallas_call | solution.py:455
  204.5 0.0 copy-start.7
  204.5 0.0 copy-start.6
  204.5 5.6 %fusion.2 = bf16[256,4096]{1,0:T(8,128)(2,1)} fusion(f32[256,4096]{1,0:T(8,128)S(1)} %fusion.6, bf16[256,512]{0,1:T(8,128)(2,1)S(1)} %bitcast.45, bf16[256,4096]{1,0:T(8,128)(2,1)S(1)} %get-tuple-element.12, bf16[512,10752]{1,0:T(8,128)(2,1)} %bitcast.40, bf16[1,256,4096]{2,1,0:T(8,128)(2,1)S(1)} %get-tuple-element.13), kind=kOutput, calls=%fused_computation.3 | convolution fusion | flops 1081081856 | bytes 14942208 | tf_op jit(solution)/shard_map/dot_general | solution.py:515
  210.1 0.0 copy-done.7
  210.1 1.0 copy.19
  211.1 0.0 copy-done.6
  211.1 1.0 copy.20
  212.1 0.8 copy.21
  212.9 0.7 copy.22
  (5 shorter events, 0.1 us)
Async XLA Ops:
  2.0 1.2 copy-start
  3.3 0.9 copy-start.1
  4.2 78.9 %copy-start.5 = (bf16[256,4096]{1,0:T(8,128)(2,1)S(1)}, bf16[256,4096]{1,0:T(8,128)(2,1)}, u32[]{:S(2)}) copy-start(bf16[256,4096]{1,0:T(8,128)(2,1)} %tokens.1) | copy-start | bytes 6291460
  81.6 5.6 %copy-start.4 = (bf16[8,64,10752]{2,1,0:T(8,128)(2,1)S(1)}, bf16[8,64,10752]{2,1,0:T(8,128)(2,1)}, u32[]{:S(2)}) copy-start(bf16[8,64,10752]{2,1,0:T(8,128)(2,1)} %get-tuple-element.14) | copy-start | bytes 33030148
  88.5 0.8 copy-start.3
  89.5 5.8 %collective-permute-start = (bf16[256,256]{0,1:T(8,128)(2,1)S(1)}, bf16[256,256]{0,1:T(8,128)(2,1)S(1)}, u32[]{:S(2)}, u32[]{:S(2)}) collective-permute-start(bf16[256,256]{0,1:T(8,128)(2,1)S(1)} %pad_maximum_fusion.1), channel_id=1, source_target_pairs={{0,1},{1,0},{2,3},{3,2},{4,5},{5,4},{6,7},{7,6},{8,9},{9,8},{10,11... | collective-permute-start | bytes 393224 | tf_op jit(solution)/shard_map/ppermute | solution.py:507
  95.4 1.3 copy-start.2
  204.5 5.7 %copy-start.7 = (f32[64,4096]{1,0:T(8,128)S(1)}, f32[64,4096]{1,0:T(8,128)}, u32[]{:S(2)}) copy-start(f32[64,4096]{1,0:T(8,128)} %get-tuple-element.15) | copy-start | bytes 3145732
  204.5 6.6 %copy-start.6 = (f32[64,4096]{1,0:T(8,128)S(1)}, f32[64,4096]{1,0:T(8,128)}, u32[]{:S(2)}) copy-start(f32[64,4096]{1,0:T(8,128)} %get-tuple-element.16) | copy-start | bytes 3145732

commit v2 on v0

v2 whole, which is shorter than its diff:
```python
import functools
import math

import jax
import jax.numpy as jnp
from jax import lax
from jax.experimental import pallas as pl
from jax.experimental.pallas import tpu as pltpu
from jax.sharding import PartitionSpec as P

D = 8192
QW = 4096
KV = 1024
R = 64

SCALE = 2.0
CLIP_RMS = 0.5
MESH = pl.DeviceIdType.MESH
PIECE = 16


def dot_cols(left, right):
    return lax.dot_general(
        left, right, (((1,), (1,)), ((), ())), preferred_element_type=jnp.float32
    )


def remote(src, dst, send, recv, where):
    return pltpu.make_async_remote_copy(
        src_ref=src, dst_ref=dst, send_sem=send, recv_sem=recv, device_id=where, device_id_type=MESH
    )


def each(low, high, body):
    def run(i, carry):
        body(i)
        return carry

    lax.fori_loop(low, high, run, 0)


def greet(z, nz, pairs, t, nt, x_partner):
    barrier = pltpu.get_barrier_semaphore()

    def signal(where):
        pl.semaphore_signal(barrier, inc=1, device_id=where, device_id_type=MESH)

    left, right, core = pairs

    @pl.when(z > 0)
    def _():
        signal({"dp": left})

    @pl.when(z < nz - 1)
    def _():
        signal({"dp": right})

    signal({"dp": core})
    if x_partner is not None:
        signal({"groups": x_partner})
    for d in range(nt - 1):
        signal({"tensor": lax.rem(t + 1 + d, nt)})
    always = 1 + (x_partner is not None) + nt - 1
    ends = jnp.where(z > 0, 1, 0) + jnp.where(z < nz - 1, 1, 0)
    pl.semaphore_wait(barrier, always + ends)


def kernel(
    n_dp, nt, tile, col,
    mine, ids, tokens, cq, cv, wq, wv,
    input_grad, aq, av, bq, bv,
    full, own, from_core, from_z, parts, wq_buf, wv_buf, out_buf,
    rk_out, rk_in, rk, spread, sq_out, sq_in,
    w_sem, l_sem, own_send, own_recv, z_send, z_recv, x_send, x_recv, c_send, c_recv,
    p_send, p_recv, r_send, r_recv, k_send, k_recv, s_send, s_recv, n_send, n_recv,
):
    nz = n_dp // 2
    me = lax.axis_index("dp")
    g = lax.axis_index("groups")
    t = lax.axis_index("tensor")
    z, c = me // 2, lax.rem(me, 2)
    other = 1 - g
    core = 2 * z + 1 - c
    left, right = me - 2, me + 2
    half = R // 2
    npiece = half // PIECE
    nsum = R // PIECE
    feat, query, value = tokens.shape[1], cq.shape[1], cv.shape[1]
    f32, bf = jnp.float32, jnp.bfloat16

    def rows(which, p):
        return pl.ds(pl.multiple_of(which * half + p * PIECE, PIECE), PIECE)

    per = feat // tile
    total, away = nt * per, (nt - 1) * per

    def tiles(i, slot):
        peer = lax.rem(t + 1 + i // per, nt)
        at = pl.ds(pl.multiple_of(peer * feat + lax.rem(i, per) * tile, tile), tile)
        return (
            pltpu.make_async_copy(wq.at[at], wq_buf.at[slot], w_sem.at[0, slot]),
            pltpu.make_async_copy(wv.at[at], wv_buf.at[slot], w_sem.at[1, slot]),
        )

    def p_copy(i):
        at = pl.ds(pl.multiple_of(lax.rem(i, per) * tile, tile), tile)
        peer = lax.rem(t + 1 + i // per, nt)
        return remote(
            out_buf.at[i], parts.at[i // per, :, at], p_send.at[i], p_recv.at[i], {"tensor": peer}
        )

    def step(i, carry):
        slot = lax.rem(i, 2)
        for copy in tiles(i, slot):
            copy.wait()

        @pl.when(i + 1 < total)
        def _():
            for copy in tiles(i + 1, 1 - slot):
                copy.start()

        got = dot_cols(cq[...], wq_buf[slot]) + dot_cols(cv[...], wv_buf[slot])
        got = got.astype(bf)

        @pl.when(i < away)
        def _():
            out_buf[i] = got
            p_copy(i).start()

        @pl.when(i >= away)
        def _():
            at = pl.ds(pl.multiple_of(lax.rem(i, per) * tile, tile), tile)
            input_grad[:, at] = got

        return carry

    def frozen(part):
        lax.fori_loop(part * total // nz, (part + 1) * total // nz, step, 0)

    for copy in tiles(0, 0):
        copy.start()

    greet(z, nz, (left, right, core), t, nt, other)

    def dest(way, j):
        return z + (1 - 2 * way) * j

    def goes(way, j):
        return jnp.logical_and(dest(way, j) >= 0, dest(way, j) <= nz - 1)

    def far(way, k):
        return z - (1 - 2 * way) * k

    def there(way, k):
        return jnp.logical_and(far(way, k) >= 0, far(way, k) <= nz - 1)

    def ahead(way):
        return {"dp": me + 2 * (1 - 2 * way)}

    def z_copy(way, k, p):
        at = full.at[2 * far(way, k) + c, rows(g, p)]
        return remote(at, at, z_send.at[way, k, p], z_recv.at[way, k, p], ahead(way))

    def z_arrival(way, k, p):
        at = full.at[2 * far(way, k + 1) + c, rows(g, p)]
        return remote(at, at, z_send.at[way, k, p], z_recv.at[way, k, p], ahead(way))

    def x_copy(way, k, p, arriving):
        at = full.at[2 * far(way, k + 1) + c, rows(other if arriving else g, p)]
        return remote(at, at, x_send.at[way, k, p], x_recv.at[way, k, p], {"groups": other})

    def c_copy(which, way, k, p, arriving):
        slot = 2 * far(way, k + 1) + (1 - c if arriving else c)
        at = full.at[slot, rows(g if which == 0 else other, p)]
        return remote(
            at, at, c_send.at[which, way, k, p], c_recv.at[which, way, k, p], {"dp": core}
        )

    def sends(way, k):
        return jnp.logical_and(there(way, k), goes(way, 1))

    def both(cond, body):
        def one(way):
            @pl.when(cond(way))
            def _():
                body(way)

        each(0, 2, one)

    def pieces(cond, body):
        each(0, npiece, lambda p: both(cond, lambda way: body(way, p)))

    local = pltpu.make_async_copy(mine, full.at[me], l_sem)
    local.start()
    local.wait()
    pieces(lambda way: sends(way, 0), lambda way, p: z_copy(way, 0, p).start())
    own_out = remote(mine, full.at[me], own_send, own_recv, {"dp": core})
    own_out.start()
    own_in = remote(mine, full.at[core], own_send, own_recv, {"dp": core})

    def arrive(k):
        def here(way):
            return there(way, k + 1)

        def from_line(way, p):
            z_arrival(way, k, p).wait_recv()

            @pl.when(sends(way, k + 1))
            def _():
                z_copy(way, k + 1, p).start()

            x_copy(way, k, p, False).start()
            c_copy(0, way, k, p, False).start()

        def from_x(way, p):
            x_copy(way, k, p, True).wait_recv()
            c_copy(1, way, k, p, False).start()

        def from_pair(way, p):
            for which in range(2):
                c_copy(which, way, k, p, True).wait_recv()

        pieces(here, from_line)
        pieces(here, from_x)
        pieces(here, from_pair)

    def k_copy(zt, d):
        return remote(
            rk_out.at[zt], rk_in.at[d, zt], k_send.at[zt, d], k_recv.at[zt, d],
            {"tensor": lax.rem(t + 1 + d, nt)},
        )

    def partial(zt):
        def product(first, width, right_ref, spans):
            wide = min(512, width)

            def run(i, acc):
                at = i * wide
                stack = [
                    full[2 * zt + s, :, pl.ds(pl.multiple_of(first + j * width + at, 128), wide)]
                    for s in range(2)
                    for j in range(spans)
                ]
                cols = pl.ds(pl.multiple_of(at, 128), wide)
                return acc + dot_cols(jnp.concatenate(stack, axis=0), right_ref[:, cols])

            zero = jnp.zeros((2 * spans * R, tokens.shape[0]), f32)
            return lax.fori_loop(0, width // wide, run, zero)

        h = product(0, feat, tokens, 2)
        gq = product(2 * feat, query, cq, 1)
        gv = product(2 * feat + query, value, cv, 1)
        two = []
        for s in range(2):
            rank = jnp.concatenate(
                [gq[s * R : (s + 1) * R], gv[s * R : (s + 1) * R], h[2 * s * R : 2 * (s + 1) * R]],
                axis=0,
            )
            two.append(jnp.where(ids[...] == 2 * zt + s, rank, 0.0))
        rk_out[zt] = (two[0] + two[1]).astype(bf)
        for d in range(nt - 1):
            k_copy(zt, d).start()

    def core_copy(zt):
        return remote(
            own.at[2 * zt + 1 - c], from_core.at[zt], s_send.at[zt], s_recv.at[zt], {"dp": core}
        )

    def contribute(zt):
        summed = rk_out[zt].astype(f32)
        for d in range(nt - 1):
            k_copy(zt, d).wait_recv()
            summed = summed + rk_in[d, zt].astype(f32)
        rk[...] = summed.astype(bf)
        masked = []
        for s in range(2):
            keep = jnp.where(ids[...] == 2 * zt + s, rk[...].astype(f32), 0.0).astype(bf)
            masked.append(keep)
            at = pl.ds(pl.multiple_of((2 * zt + s) * R, R), R)
            spread[0, at, :] = keep[:R]
            spread[1, at, :] = keep[R : 2 * R]

        def over(first, width, right_ref, low, spans):
            wide = min(col, width)
            lhs = jnp.concatenate([m[low * R : (low + spans) * R] for m in masked], axis=0)

            def run(i, carry):
                at = pl.multiple_of(i * wide, 128)
                got = jnp.dot(lhs, right_ref[:, pl.ds(at, wide)], preferred_element_type=f32)
                got = got.astype(bf)
                for s in range(2):
                    for j in range(spans):
                        cols = pl.ds(pl.multiple_of(first + j * width + at, 128), wide)
                        low_row = (s * spans + j) * R
                        own[2 * zt + s, :, cols] = got[low_row : low_row + R]
                return carry

            lax.fori_loop(0, width // wide, run, 0)

        over(0, feat, tokens, 0, 2)
        over(2 * feat, query, cq, 2, 1)
        over(2 * feat + query, value, cv, 3, 1)
        core_copy(zt).start()

    def pair_sum(zt):
        core_copy(zt).wait_recv()
        mine_at = 2 * zt + c

        def add(p):
            at = pl.ds(pl.multiple_of(p * PIECE, PIECE), PIECE)
            own[mine_at, at] = (
                own[mine_at, at].astype(f32) + from_core[zt, at].astype(f32)
            ).astype(bf)

        each(0, nsum, add)

    def slot_of(way, zt, last):
        return zt + jnp.where(last, way * (nz - zt), 0)

    def r_copy(way, j, p):
        zt = dest(way, j)
        at = pl.ds(pl.multiple_of(p * PIECE, PIECE), PIECE)
        return remote(
            own.at[2 * zt + c, at], from_z.at[slot_of(way, zt, j == 1), at],
            r_send.at[way, zt, p], r_recv.at[way, zt, p], ahead(way),
        )

    def r_arrival(way, j, p):
        zt = dest(way, j)
        at = pl.ds(pl.multiple_of(p * PIECE, PIECE), PIECE)
        ref = from_z.at[slot_of(way, zt, j == 0), at]
        return remote(ref, ref, r_send.at[way, zt, p], r_recv.at[way, zt, p], ahead(way))

    def start_sum(way, j, p):
        before = (j - 1) * nsum + p - 2

        @pl.when(before >= 0)
        def _():
            r_copy(way, before // nsum + 1, lax.rem(before, nsum)).wait_send()

        r_copy(way, j, p).start()

    def first_of(way):
        return z == way * (nz - 1)

    frozen(0)
    own_in.wait_recv()
    partial(z)

    def distance(k):
        def on(way):
            return goes(way, k)

        def gradients(way):
            contribute(dest(way, k))

        def send_first(way):
            each(0, nsum, lambda p: start_sum(way, k, p))

        arrive(k - 1)
        both(on, lambda way: partial(dest(way, k)))
        both(on, gradients)
        both(on, lambda way: pair_sum(dest(way, k)))
        both(lambda way: jnp.logical_and(on(way), first_of(way)), send_first)
        frozen(k)

    each(1, nz, distance)
    contribute(z)
    pair_sum(z)

    def finish(i, carry):
        p_copy(i).wait_recv()
        return carry

    lax.fori_loop(0, away, finish, 0)

    def add_adapters(i, carry):
        wide = min(512, feat)
        at = pl.multiple_of(i * wide, 128)
        rows_in = (((0,), (0,)), ((), ()))
        sums = input_grad[:, pl.ds(at, wide)].astype(f32)
        for d in range(nt - 1):
            sums = sums + parts[d, :, pl.ds(at, wide)].astype(f32)
        for j in range(2):
            cols = pl.ds(pl.multiple_of(j * feat + at, 128), wide)
            maps = full[:, :, cols].reshape(n_dp * R, wide)
            sums = sums + SCALE * lax.dot_general(
                spread[j], maps, rows_in, preferred_element_type=f32
            )
        input_grad[:, pl.ds(at, wide)] = sums.astype(bf)
        return carry

    lax.fori_loop(0, feat // min(512, feat), add_adapters, 0)

    def pass_on(time):
        def left_to_go(way):
            return time - 2 * (z + way * (nz - 1 - 2 * z))

        def add(way, p):
            j = left_to_go(way)
            r_arrival(way, j, p).wait_recv()
            at = pl.ds(pl.multiple_of(p * PIECE, PIECE), PIECE)
            zt = dest(way, j)
            own[2 * zt + c, at] = (
                own[2 * zt + c, at].astype(f32) + from_z[zt, at].astype(f32)
            ).astype(bf)
            start_sum(way, j, p)

        def inner(way):
            j = left_to_go(way)
            valid = jnp.logical_and(j >= 1, goes(way, j))
            return jnp.logical_and(valid, jnp.logical_not(first_of(way)))

        each(0, nsum, lambda p: both(inner, lambda way: add(way, p)))

    each(1, 2 * nz - 2, pass_on)

    places = ((aq, 0, feat), (av, feat, feat), (bq, 2 * feat, query), (bv, 2 * feat + query, value))

    def collect(p, norm):
        at = pl.ds(pl.multiple_of(p * PIECE, PIECE), PIECE)
        both(lambda way: there(way, 1), lambda way: r_arrival(way, 0, p).wait_recv())
        for ref, first, width in places:
            ref[at, :] = own[me, at, pl.ds(first, width)].astype(f32)

        def add(way):
            for ref, first, width in places:
                cols = pl.ds(first, width)
                ref[at, :] += from_z[slot_of(way, z, True), at, cols].astype(f32)

        both(lambda way: there(way, 1), add)
        for ref, _, _ in places:
            sums = SCALE * ref[at, :]
            ref[at, :] = sums
            norm = norm + jnp.sum(sums * sums, axis=(0, 1), keepdims=True)
        return norm

    norm = lax.fori_loop(0, nsum, collect, jnp.zeros((1, 1), f32))
    sq_out[...] = jnp.broadcast_to(norm, sq_out.shape)

    def n_copy(d):
        return remote(
            sq_out, sq_in.at[d], n_send.at[d], n_recv.at[d], {"tensor": lax.rem(t + 1 + d, nt)}
        )

    for d in range(nt - 1):
        n_copy(d).start()
    norm = sq_out[0:1, 0:1]
    for d in range(nt - 1):
        n_copy(d).wait_recv()
        norm = norm + sq_in[d, 0:1, 0:1]
    entries = float(R * (2 * D + QW + KV))
    factor = jnp.minimum(1.0, CLIP_RMS * math.sqrt(entries) / jnp.sqrt(norm + 1e-06))
    for ref, _, _ in places:
        ref[...] = ref[...] * factor

    for d in range(nt - 1):
        n_copy(d).wait_send()
    def pair_left(zt):
        core_copy(zt).wait_send()
        for d in range(nt - 1):
            k_copy(zt, d).wait_send()

    each(0, nz, pair_left)
    own_out.wait_send()

    def gather_left(k):
        def shared(way, p):
            for which in range(2):
                c_copy(which, way, k, p, False).wait_send()
            x_copy(way, k, p, False).wait_send()

        pieces(lambda way: there(way, k + 1), shared)
        pieces(lambda way: sends(way, k), lambda way, p: z_copy(way, k, p).wait_send())

    each(0, nz - 1, gather_left)

    def sums_left(j):
        def last(way):
            return jnp.logical_and(goes(way, j), jnp.logical_not(goes(way, j + 1)))

        each(nsum - 2, nsum, lambda p: both(last, lambda way: r_copy(way, j, p).wait_send()))

    each(1, nz, sums_left)

    def left_all(i, carry):
        p_copy(i).wait_send()
        return carry

    lax.fori_loop(0, away, left_all, 0)


def on_device(
    n_dp, nt,
    tokens, tenant_ids, cot_query, cot_value, w_query, w_value, a_query, a_value, b_query, b_value
):
    bf, f32 = jnp.bfloat16, jnp.float32
    feat, query, value = tokens.shape[1], cot_query.shape[1], cot_value.shape[1]
    rows = tokens.shape[0]
    mine = jnp.concatenate([a_query[0], a_value[0], b_query[0], b_value[0]], axis=1)
    width = mine.shape[1]
    tile = min(256, feat)
    nz = n_dp // 2
    npiece, nsum = R // 2 // PIECE, R // PIECE
    away = (nt - 1) * (feat // tile)
    hbm = pl.BlockSpec(memory_space=pl.ANY)
    vmem = pl.BlockSpec(memory_space=pltpu.VMEM)
    dma = pltpu.SemaphoreType.DMA
    outs = pl.pallas_call(
        functools.partial(kernel, n_dp, nt, tile, 1024),
        out_shape=(jax.ShapeDtypeStruct((rows, feat), bf),)
        + tuple(jax.ShapeDtypeStruct((R, w), f32) for w in (feat, feat, query, value)),
        in_specs=[hbm, vmem, vmem, vmem, vmem, hbm, hbm],
        out_specs=(vmem,) * 5,
        scratch_shapes=[
            pltpu.VMEM((n_dp, R, width), bf),
            pltpu.VMEM((n_dp, R, width), bf),
            pltpu.VMEM((nz, R, width), bf),
            pltpu.VMEM((nz + 1, R, width), bf),
            pltpu.VMEM((nt - 1, rows, feat), bf),
            pltpu.VMEM((2, tile, query), bf),
            pltpu.VMEM((2, tile, value), bf),
            pltpu.VMEM((away, rows, tile), bf),
            pltpu.VMEM((nz, 4 * R, rows), bf),
            pltpu.VMEM((nt - 1, nz, 4 * R, rows), bf),
            pltpu.VMEM((4 * R, rows), bf),
            pltpu.VMEM((2, n_dp * R, rows), bf),
            pltpu.VMEM((8, 128), f32),
            pltpu.VMEM((nt - 1, 8, 128), f32),
            dma((2, 2)),
            dma,
            dma,
            dma,
            dma((2, nz - 1, npiece)),
            dma((2, nz - 1, npiece)),
            dma((2, nz - 1, npiece)),
            dma((2, nz - 1, npiece)),
            dma((2, 2, nz - 1, npiece)),
            dma((2, 2, nz - 1, npiece)),
            dma((away,)),
            dma((away,)),
            dma((2, nz, nsum)),
            dma((2, nz, nsum)),
            dma((nz, nt - 1)),
            dma((nz, nt - 1)),
            dma((nz,)),
            dma((nz,)),
            dma((nt - 1,)),
            dma((nt - 1,)),
        ],
        compiler_params=pltpu.CompilerParams(
            collective_id=0, has_side_effects=True, vmem_limit_bytes=57 * 2**20
        ),
    )(mine, tenant_ids, tokens, cot_query, cot_value, w_query, w_value)
    return (outs[0],) + tuple(out[None] for out in outs[1:])


def solution(mesh):
    n_dp, nt = mesh.shape["dp"], mesh.shape["tensor"]
    in_specs = (
        P(("groups", "dp"), "tensor"),
        P(("groups", "dp"), None),
        P(("groups", "dp"), "tensor"),
        P(("groups", "dp"), "tensor"),
        P(None, "tensor"),
        P(None, "tensor"),
        P("dp", None, "tensor"),
        P("dp", None, "tensor"),
        P("dp", None, "tensor"),
        P("dp", None, "tensor"),
    )
    out_specs = (
        P(("groups", "dp"), "tensor"),
        P(("groups", "dp"), None, "tensor"),
        P(("groups", "dp"), None, "tensor"),
        P(("groups", "dp"), None, "tensor"),
        P(("groups", "dp"), None, "tensor"),
    )
    return jax.shard_map(
        functools.partial(on_device, n_dp, nt),
        mesh=mesh, in_specs=in_specs, out_specs=out_specs, check_vma=False,
    )
```

time: 382 us -> 237 us (0.62)
  the two profiles are of different devices: /device:TPU:16 before, /device:TPU:0 now
where the time goes in v2:
time: 237 us; the launch traced here: 236 us
  Pallas kernels  227 us (96%)
  local copies, waits for them, and re-layouts  6.68 us (3%)
  other arithmetic  2.49 us (1%)
    pallas_call x1, Pallas kernels, on_device(): pl.pallas_call(functools.partial(kernel, n_dp, nt, tile, 1024), out_shape...  227 us
    unnamed x13, local copies, waits for them, and re-layouts  6.68 us

profile of v2, /device:TPU:0, one launch (start us, length us, event | category | flops | bytes accessed | tf_op | source)
XLA Modules:
  0.0 236.4 jit_solution(15894329404068527434)
XLA Ops:
  0.6 2.5 %pad_maximum_fusion.mine = bf16[64,10752]{1,0:T(8,128)(2,1)} fusion(bf16[64,512]{1,0:T(8,128)(2,1)} %bitcast.15, bf16[64,2048]{1,0:T(8,128)(2,1)} %bitcast.13, bf16[64,4096]{1,0:T(8,128)(2,1)} %bitcast.11, bf16[64,4096]{1,0:T(8,128)(2,1)} %bitcast.12), kind=kLoop, calls=%fused_computation | loop fusion | flops 5505024 | bytes 2752512 | tf_op jit(solution)/shard_map/concatenate | solution.py:500
  3.1 226.6 %shard_map.137 = (bf16[256,4096]{1,0:T(8,128)(2,1)}, f32[64,4096]{1,0:T(8,128)}, f32[64,4096]{1,0:T(8,128)}, f32[64,2048]{1,0:T(8,128)}, f32[64,512]{1,0:T(8,128)}) custom-call(bf16[64,10752]{1,0:T(8,128)(2,1)} %pad_maximum_fusion.mine, s32[1,256]{1,0:T(1,128)} %ids.1, bf16[256,4096]{1,0:T(8,128)(2,1)} %tokens.1, bf16[256,2048]{1,0:T(8,128)(2,1)} %cq.1, ...), custom_call_target="tpu_custom_call" | custom-call | tf_op jit(solution)/shard_map/pallas_call | solution.py:509
  229.7 0.0 copy-start.1
  229.7 0.0 copy-start
  229.7 3.3 %copy.20 = bf16[256,4096]{1,0:T(8,128)(2,1)} copy(bf16[256,4096]{1,0:T(8,128)(2,1)} %get-tuple-element.20) | data formatting | bytes 4194304
  233.0 0.0 copy-done.1
  233.0 0.0 copy-start.2
  233.0 0.0 copy-start.3
  233.0 1.0 copy.21
  234.0 0.0 copy-done
  234.0 1.0 copy.22
  235.0 0.0 copy-done.2
  235.0 0.8 copy.23
  235.8 0.0 copy-done.3
  235.8 0.7 copy.24
Async XLA Ops:
  229.7 3.3 %copy-start.1 = (f32[64,4096]{1,0:T(8,128)S(1)}, f32[64,4096]{1,0:T(8,128)}, u32[]{:S(2)}) copy-start(f32[64,4096]{1,0:T(8,128)} %get-tuple-element.11) | copy-start | bytes 3145732
  229.7 4.3 %copy-start = (f32[64,4096]{1,0:T(8,128)S(1)}, f32[64,4096]{1,0:T(8,128)}, u32[]{:S(2)}) copy-start(f32[64,4096]{1,0:T(8,128)} %get-tuple-element.12) | copy-start | bytes 3145732
  233.0 1.9 copy-start.2
  233.0 2.7 %copy-start.3 = (f32[64,512]{1,0:T(8,128)S(1)}, f32[64,512]{1,0:T(8,128)}, u32[]{:S(2)}) copy-start(f32[64,512]{1,0:T(8,128)} %get-tuple-element.14) | copy-start | bytes 393220

commit v3 on v1

--- a/solution.py
+++ b/solution.py
@@ -177,7 +177,7 @@
 
         return carry
 
-    lax.fori_loop(0, total, step, 0)
+    lax.fori_loop(0, total // 2, step, 0)
 
     def from_x(k):
         for p in range(npiece):
@@ -187,6 +187,7 @@
                     x_copy(way, k, p, True).wait_recv()
                     c_copy(1, way, k, p, False).start()
 
+    cuts = [total // 2 + (total - total // 2) * n // npiece for n in range(npiece + 1)]
     for k in range(nz - 1):
         for p in range(npiece):
             for way in range(2):
@@ -199,6 +200,8 @@
                             z_copy(way, k + 1, p, False).start()
                     x_copy(way, k, p, False).start()
                     c_copy(0, way, k, p, False).start()
+            if k == 0:
+                lax.fori_loop(cuts[p], cuts[p + 1], step, 0)
         if k > 0:
             from_x(k - 1)
     from_x(nz - 2)
@@ -373,16 +376,12 @@
         contribute(2 * zt + 1 - c)
         core_copy(zt).start()
         contribute(2 * zt + c)
-        if n == 1:
-            for earlier in order[:2]:
-                pair_sum(earlier)
-            for p in range(npiece):
-                for way in range(2):
-                    @pl.when(z == 0 if way == 0 else z == nz - 1)
-                    def _(way=way, p=p):
-                        pass_on(way, 0, p)
-        elif n > 1:
-            pair_sum(zt)
+        pair_sum(zt)
+        if n < 2:
+            @pl.when(z == 0 if n == 0 else z == nz - 1)
+            def _(n=n):
+                for p in range(npiece):
+                    pass_on(n, 0, p)
 
     for tau in range(1, nz - 1):
         for p in range(npiece):

time: 214 us -> 203 us (0.949)
  Pallas kernels: 185 us -> 173 us
    pallas_call x1, Pallas kernels: 77.4 us -> 64 us  [gather(): pl.pallas_call(functools.partial(gather_kernel, n_dp, nt, tile), out_shap...]
where the time goes in v3:
time: 203 us; the launch traced here: 202 us
  Pallas kernels  173 us (85%)
  matrix products  14.3 us (7%)
  local copies, waits for them, and re-layouts  5.75 us (3%)
  waiting for transfers between devices  4.24 us (2%)
    pallas_call x1, Pallas kernels, grads(): pl.pallas_call(functools.partial(grads_kernel, n_dp, nt, 1024), out_shape...  109 us
    pallas_call x1, Pallas kernels, gather(): pl.pallas_call(functools.partial(gather_kernel, n_dp, nt, tile), out_shap...  64 us
    dot_general x4, matrix products, dot_cols(): lax.dot_general(left, right, (((1,), (1,)), ((), ())), preferred_element_...  7.38 us
    unnamed x20, local copies, waits for them, and re-layouts  5.74 us
    dot_general x1, matrix products, on_device(): jnp.dot(spread(ranks[:, R:2 * R]), flat_av, preferred_element_type=f32)  5.64 us
    ppermute x1, waiting for transfers between devices, on_device(): got = lax.ppermute(part, 'tensor', [(0, 1), (1, 0)])  4.24 us
  transfers between devices with their start and end apart: 1, of which 1 were waited for; matrix products, arithmetic and copies ran while one was open for 0% of the time, Pallas kernels for 0%

profile of v3, /device:TPU:16, one launch (start us, length us, event | category | flops | bytes accessed | tf_op | source)
XLA Modules:
  0.0 201.8 jit_solution(17557873142118781065)
XLA Ops:
  0.6 1.4 pad_maximum_fusion.mine
  2.0 0.0 copy-start
  2.1 1.2 copy-done
  3.3 0.0 copy-start.1
  3.3 0.9 copy-done.1
  4.2 0.0 copy-start.5
  4.2 64.0 %shard_map.137 = (bf16[8,64,10752]{2,1,0:T(8,128)(2,1)}, bf16[256,4096]{1,0:T(8,128)(2,1)S(1)}, bf16[1,256,4096]{2,1,0:T(8,128)(2,1)S(1)}) custom-call(bf16[64,10752]{1,0:T(8,128)(2,1)S(1)} %pad_maximum_fusion.mine, bf16[256,2048]{1,0:T(8,128)(2,1)S(1)} %copy-done, bf16[256,512]{1,0:T(8,128)(2,1)S(1)} %copy-done.1, bf16[8192,2048]{1,0:T(8,128)(2,1)} %wq.1, ...), custom_call_target="tpu_custom_call" | custom-call | tf_op jit(solution)/shard_map/pallas_call | solution.py:246
  68.3 0.0 copy-start.4
  68.3 1.5 fusion.12
  69.8 0.0 copy-done.5
  69.8 3.8 %fusion.8 = f32[512,256]{1,0:T(8,128)S(1)} fusion(bf16[256,4096]{1,0:T(8,128)(2,1)S(1)} %copy-done.5, bf16[512,10752]{1,0:T(8,128)(2,1)} %bitcast.39), kind=kOutput, calls=%fused_computation.10 | convolution fusion | flops 1073741824 | bytes 6815744 | tf_op jit(solution)/shard_map/dot_general | solution.py:23
  73.7 0.2 copy-done.4
  73.8 1.3 fusion.4
  75.1 0.0 copy-start.3
  75.1 0.7 fusion.10
  75.9 0.0 copy-done.3
  75.9 0.2 select_reduce_fusion.3
  76.1 1.6 collective-permute-start
  77.7 4.2 %collective-permute-done = bf16[256,256]{0,1:T(8,128)(2,1)S(1)} collective-permute-done((bf16[256,256]{0,1:T(8,128)(2,1)S(1)}, bf16[256,256]{0,1:T(8,128)(2,1)S(1)}, u32[]{:S(2)}, u32[]{:S(2)}) %collective-permute-start) | collective-permute-done | bytes 131104 | tf_op jit(solution)/shard_map/ppermute | solution.py:506
  82.0 0.0 copy-start.2
  82.1 1.3 fusion.6
  83.3 0.0 copy-done.2
  83.3 109.4 %shard_map.138 = (f32[64,4096]{1,0:T(8,128)}, f32[64,4096]{1,0:T(8,128)}, f32[64,2048]{1,0:T(8,128)S(1)}, f32[64,512]{1,0:T(8,128)S(1)}) custom-call(bf16[256,256]{1,0:T(8,128)(2,1)S(1)} %bitcast.34, s32[1,256]{1,0:T(1,128)S(1)} %copy-done.3, bf16[256,4096]{1,0:T(8,128)(2,1)} %tokens.1, bf16[256,2048]{1,0:T(8,128)(2,1)} %cq.3, bf16[256,512]{1,0:T(8,128)(2,1)S(1)} %copy-done.2), custom_call_target="tpu_custom_call" | custom-call | tf_op jit(solution)/shard_map/pallas_call | solution.py:454
  192.7 0.0 copy-start.7
  192.7 0.0 copy-start.6
  192.7 5.6 %fusion.2 = bf16[256,4096]{1,0:T(8,128)(2,1)} fusion(f32[256,4096]{1,0:T(8,128)S(1)} %fusion.6, bf16[256,512]{0,1:T(8,128)(2,1)S(1)} %bitcast.45, bf16[256,4096]{1,0:T(8,128)(2,1)S(1)} %get-tuple-element.12, bf16[512,10752]{1,0:T(8,128)(2,1)} %bitcast.40, bf16[1,256,4096]{2,1,0:T(8,128)(2,1)S(1)} %get-tuple-element.13), kind=kOutput, calls=%fused_computation.3 | convolution fusion | flops 1081081856 | bytes 14942208 | tf_op jit(solution)/shard_map/dot_general | solution.py:514
  198.4 0.0 copy-done.7
  198.4 1.0 copy.19
  199.3 0.0 copy-done.6
  199.3 1.0 copy.20
  200.3 0.8 copy.21
  201.1 0.7 copy.22
  (5 shorter events, 0.1 us)
Async XLA Ops:
  2.0 1.2 copy-start
  3.3 0.9 copy-start.1
  4.2 65.6 %copy-start.5 = (bf16[256,4096]{1,0:T(8,128)(2,1)S(1)}, bf16[256,4096]{1,0:T(8,128)(2,1)}, u32[]{:S(2)}) copy-start(bf16[256,4096]{1,0:T(8,128)(2,1)} %tokens.1) | copy-start | bytes 6291460
  68.3 5.6 %copy-start.4 = (bf16[8,64,10752]{2,1,0:T(8,128)(2,1)S(1)}, bf16[8,64,10752]{2,1,0:T(8,128)(2,1)}, u32[]{:S(2)}) copy-start(bf16[8,64,10752]{2,1,0:T(8,128)(2,1)} %get-tuple-element.14) | copy-start | bytes 33030148
  75.1 0.8 copy-start.3
  76.1 5.8 %collective-permute-start = (bf16[256,256]{0,1:T(8,128)(2,1)S(1)}, bf16[256,256]{0,1:T(8,128)(2,1)S(1)}, u32[]{:S(2)}, u32[]{:S(2)}) collective-permute-start(bf16[256,256]{0,1:T(8,128)(2,1)S(1)} %pad_maximum_fusion.1), channel_id=1, source_target_pairs={{0,1},{1,0},{2,3},{3,2},{4,5},{5,4},{6,7},{7,6},{8,9},{9,8},{10,11... | collective-permute-start | bytes 393224 | tf_op jit(solution)/shard_map/ppermute | solution.py:506
  82.0 1.3 copy-start.2
  192.7 5.7 %copy-start.7 = (f32[64,4096]{1,0:T(8,128)S(1)}, f32[64,4096]{1,0:T(8,128)}, u32[]{:S(2)}) copy-start(f32[64,4096]{1,0:T(8,128)} %get-tuple-element.15) | copy-start | bytes 3145732
  192.7 6.6 %copy-start.6 = (f32[64,4096]{1,0:T(8,128)S(1)}, f32[64,4096]{1,0:T(8,128)}, u32[]{:S(2)}) copy-start(f32[64,4096]{1,0:T(8,128)} %get-tuple-element.16) | copy-start | bytes 3145732
